TPU v7x, 256 devices: a whole 4x4x8 slice. The times are simulated.
256 devices in a mesh: blk: 16 (over y_hi, z), group: 16 (over x, y_lo, core).
Axes of the slice: x: 4, y: 4 (y_hi: 2, y_lo: 2; y = y_hi * 2 + y_lo), z: 8, core: 2. Of those that a mesh axis runs over, the one named last changes fastest.
Arguments:
- images: bfloat16 [163840, 1152], P(('blk', 'group')), may hold values from -0.1796875 to 0.1796875
- texts: bfloat16 [163840, 1152], P(('blk', 'group')), may hold values from -0.1796875 to 0.1796875
- image_ids: int32 [163840], P(('blk', 'group')), may hold values from 0 to 255
- text_ids: int32 [163840], P(('blk', 'group')), may hold values from 0 to 255
- logit_scale: float32 [1], replicated, may hold values from 5 to 12
- logit_bias: float32 [1], replicated, may hold values from -4 to -1
Outputs:
- row_loss: float32 [163840], P(('blk', 'group'))
- image_grad: float32 [163840, 1152], P(('blk', 'group'))
- text_grad: float32 [163840, 1152], P(('blk', 'group'))
All inputs are finite; a program needn't handle non-finite values.
Results may differ from a plain program's by a relative error of at most 0.0052.
Values may be sent and summed in bfloat16 or wider, within the bound.
No kernel may reach another device: no remote copies, remote signals or barrier semaphores. Data moves between devices by JAX's collectives and lax.ppermute only.
A program may use at most 64 MiB of HBM per device.

v0:
```python
import jax
import jax.numpy as jnp
from jax import lax
from jax.sharding import PartitionSpec as P


def passed_along(shard, axis, by):
    devices = lax.axis_size(axis)
    return lax.ppermute(shard, axis, [(i, (i + by) % devices) for i in range(devices)])


def unit_rows(values):
    full = values.astype(jnp.float32)
    norms = jnp.sqrt(jnp.sum(full * full, axis=-1, keepdims=True) + 1e-06)
    return (full / norms, norms)


def tile_terms(image_bf, image_ids, text_bf, text_ids, scale, bias):
    logits = scale * jnp.dot(image_bf, text_bf.T, preferred_element_type=jnp.float32) + bias
    signs = jnp.where(image_ids[:, None] == text_ids[None, :], 1.0, -1.0).astype(jnp.float32)
    loss_part = jnp.sum(jax.nn.softplus(-signs * logits), axis=1)
    coef = (-signs * scale * jax.nn.sigmoid(-signs * logits)).astype(jnp.bfloat16)
    image_part = jnp.dot(coef, text_bf, preferred_element_type=jnp.float32)
    text_part = lax.dot_general(
        coef, image_bf, (((0,), (0,)), ((), ())), preferred_element_type=jnp.float32
    )
    return (loss_part, image_part, text_part.astype(jnp.bfloat16))


def shards(images, texts, image_ids, text_ids, logit_scale, logit_bias):
    rows = images.shape[0]
    image_unit, image_norm = unit_rows(images)
    text_unit, text_norm = unit_rows(texts)
    image_bf = image_unit.astype(jnp.bfloat16)
    text_bf = text_unit.astype(jnp.bfloat16)
    scale = logit_scale[0]
    bias = logit_bias[0]
    near_bf, near_ids = passed_along((text_bf, text_ids), "blk", 1)
    far_bf, far_ids = passed_along((near_bf, near_ids), "blk", 1)
    hop_bf, hop_ids = passed_along((text_bf, text_ids), "group", 1)
    own_loss, own_image, own_text = tile_terms(image_bf, image_ids, text_bf, text_ids, scale, bias)
    near_loss, near_image, near_text = tile_terms(
        image_bf, image_ids, near_bf, near_ids, scale, bias
    )
    far_loss, far_image, far_text = tile_terms(image_bf, image_ids, far_bf, far_ids, scale, bias)
    hop_loss, hop_image, hop_text = tile_terms(image_bf, image_ids, hop_bf, hop_ids, scale, bias)
    back_near = passed_along(near_text, "blk", -1)
    back_far = passed_along(far_text, "blk", -2)
    back_hop = passed_along(hop_text, "group", -1)
    row_loss = (own_loss + near_loss + far_loss + hop_loss) / (4 * rows)
    image_unit_grad = own_image + near_image + far_image + hop_image
    text_unit_grad = own_text.astype(jnp.float32) + back_near.astype(jnp.float32)
    text_unit_grad = text_unit_grad + back_far.astype(jnp.float32) + back_hop.astype(jnp.float32)
    image_grad = (
        image_unit_grad - image_unit * jnp.sum(image_unit * image_unit_grad, axis=1, keepdims=True)
    ) / image_norm
    text_grad = (
        text_unit_grad - text_unit * jnp.sum(text_unit * text_unit_grad, axis=1, keepdims=True)
    ) / text_norm
    return (row_loss, image_grad, text_grad)


def solution(mesh):
    placed = (
        P(("blk", "group"), None),
        P(("blk", "group"), None),
        P(("blk", "group")),
        P(("blk", "group")),
        P(),
        P(),
    )
    return jax.shard_map(
        shards,
        mesh=mesh,
        in_specs=placed,
        out_specs=(P(("blk", "group")), P(("blk", "group"), None), P(("blk", "group"), None)),
        check_vma=False,
    )
```

profile of v0, /device:TPU:4, one launch (start us, length us, event | category | flops | bytes accessed | tf_op | source)
XLA Modules:
  0.0 183.0 jit_solution(3614946243367088622)
XLA Ops:
  0.6 1.8 %fusion.3 = f32[640]{0:T(1024)S(1)} fusion(bf16[640,1152]{1,0:T(8,128)(2,1)} %param.7), kind=kLoop, calls=%fused_computation.17 | loop fusion | flops 2211200 | bytes 1477120 | tf_op jit(solution)/shard_map/reduce_sum | solution.py:14
  3.1 2.0 %collective-permute-start.1 = (bf16[640,1152]{1,0:T(8,128)(2,1)S(1)}, bf16[640,1152]{1,0:T(8,128)(2,1)S(1)}, u32[]{:S(2)}, u32[]{:S(2)}) collective-permute-start(bf16[640,1152]{1,0:T(8,128)(2,1)S(1)} %fusion.9), channel_id=1, source_target_pairs={{0,16},{16,32},{32,48},{48,64},{64,80},{80,96},{96,112},{112,128},... | collective-permute-start | bytes 4423688 | tf_op jit(solution)/shard_map/ppermute | solution.py:9
  5.1 1.3 collective-permute-start.4
  6.4 1.9 %collective-permute-start = (s32[640]{0:T(1024)S(1)}, s32[640]{0:T(1024)S(1)}, u32[]{:S(2)}, u32[]{:S(2)}) collective-permute-start(s32[640]{0:T(1024)S(1)} %copy-done.2), channel_id=1, source_target_pairs={{0,16},{16,32},{32,48},{48,64},{64,80},{80,96},{96,112},{112,128},... | collective-permute-start | bytes 7688 | tf_op jit(solution)/shard_map/ppermute | solution.py:9
  10.0 2.3 %fusion.4 = (f32[640]{0:T(1024)S(1)}, f32[640,640]{0,1:T(8,128)S(1)}) fusion(f32[]{:T(128)} %bitcast.22, bf16[640,1152]{1,0:T(8,128)(2,1)S(1)} %fusion.9, f32[640]{0:T(1024)S(1)} %add_sqrt_fusion.1, bf16[640,1152]{1,0:T(8,128)(2,1)S(1)} %copy-done.1, f32[]{:T(128)} %bitcast.10, s32[640]{0:T(1024)S(1)} %copy-done.2, s32[640]{0:T(1024)S(1)} %copy-done.3), kind=kOutput, calls=%fused_computation.23 | convolution fusion | flops 951254400 | bytes 4597768 | tf_op jit(solution)/shard_map/dot_general | solution.py:19
  12.4 1.6 fusion.10
  14.0 30.4 %collective-permute-done = s32[640]{0:T(1024)S(1)} collective-permute-done((s32[640]{0:T(1024)S(1)}, s32[640]{0:T(1024)S(1)}, u32[]{:S(2)}, u32[]{:S(2)}) %collective-permute-start) | collective-permute-done | bytes 2592 | tf_op jit(solution)/shard_map/ppermute | solution.py:9
  44.4 2.3 %fusion.7 = (f32[640]{0:T(1024)S(1)}, f32[640,640]{0,1:T(8,128)S(1)}) fusion(f32[]{:T(128)} %bitcast.23, bf16[640,1152]{1,0:T(8,128)(2,1)S(1)} %collective-permute-done.5, f32[640]{0:T(1024)S(1)} %add_sqrt_fusion.1, bf16[640,1152]{1,0:T(8,128)(2,1)S(1)} %copy-done.1, f32[]{:T(128)} %bitcast.15, s32[640]{0:T(1024)S(1)} %collective-permute-done.4, ...), kind=kOutput, calls=%fused_computation.26 | convolution fusion | flops 951254400 | bytes 4597768 | tf_op jit(solution)/shard_map/dot_general | solution.py:19
  46.8 1.8 convolution_convert_fusion
  48.6 12.1 %collective-permute-start.8 = (bf16[640,1152]{1,0:T(8,128)(2,1)S(1)}, bf16[640,1152]{1,0:T(8,128)(2,1)S(1)}, u32[]{:S(2)}, u32[]{:S(2)}) collective-permute-start(bf16[640,1152]{1,0:T(8,128)(2,1)S(1)} %convolution_convert_fusion), channel_id=1, source_target_pairs={{0,15},{1,0},{2,1},{3,2},{4,3},{5,4},{6,5},{7,6},{8,7},{9,8},{10,9... | collective-permute-start | bytes 4423688 | tf_op jit(solution)/shard_map/ppermute | solution.py:9
  60.8 2.3 %fusion.5 = (f32[640]{0:T(1024)S(1)}, f32[640,640]{0,1:T(8,128)S(1)}) fusion(f32[]{:T(128)} %bitcast.25, bf16[640,1152]{1,0:T(8,128)(2,1)S(1)} %collective-permute-done.1, f32[640]{0:T(1024)S(1)} %add_sqrt_fusion.1, bf16[640,1152]{1,0:T(8,128)(2,1)S(1)} %copy-done.1, f32[]{:T(128)} %bitcast.17, s32[640]{0:T(1024)S(1)} %collective-permute-done, ...), kind=kOutput, calls=%fused_computation.24 | convolution fusion | flops 951254400 | bytes 4597768 | tf_op jit(solution)/shard_map/dot_general | solution.py:19
  63.1 1.8 %convolution_convert_fusion.2 = bf16[640,1152]{1,0:T(8,128)(2,1)S(1)} fusion(f32[640,640]{0,1:T(8,128)S(1)} %get-tuple-element.10, f32[]{:T(128)} %bitcast.18, s32[640]{0:T(1024)S(1)} %copy-done.3, s32[640]{0:T(1024)S(1)} %collective-permute-done, f32[640]{0:T(1024)S(1)} %add_sqrt_fusion.1, bf16[640,1152]{1,0:T(8,128)(2,1)S(1)} %copy-done.1), kind=kOutput, calls=%fused_computation.13 | convolution fusion | flops 950353920 | bytes 4595204 | tf_op jit(solution)/shard_map/dot_general | solution.py:24
  65.0 6.3 %collective-permute-start.6 = (bf16[640,1152]{1,0:T(8,128)(2,1)S(1)}, bf16[640,1152]{1,0:T(8,128)(2,1)S(1)}, u32[]{:S(2)}, u32[]{:S(2)}) collective-permute-start(bf16[640,1152]{1,0:T(8,128)(2,1)S(1)} %convolution_convert_fusion.2), channel_id=1, source_target_pairs={{0,240},{16,0},{32,16},{48,32},{64,48},{80,64},{96,80},{112,96},{1... | collective-permute-start | bytes 4423688 | tf_op jit(solution)/shard_map/ppermute | solution.py:9
  71.2 1.6 convolution_add_fusion.1
  72.8 1.6 fusion.11
  74.5 36.4 %collective-permute-done.3 = bf16[640,1152]{1,0:T(8,128)(2,1)S(1)} collective-permute-done((bf16[640,1152]{1,0:T(8,128)(2,1)S(1)}, bf16[640,1152]{1,0:T(8,128)(2,1)S(1)}, u32[]{:S(2)}, u32[]{:S(2)}) %collective-permute-start.3) | collective-permute-done | bytes 1474592 | tf_op jit(solution)/shard_map/ppermute | solution.py:9
  110.9 2.3 %fusion.6 = (f32[640]{0:T(1024)S(1)}, f32[640,640]{0,1:T(8,128)S(1)}) fusion(f32[]{:T(128)} %bitcast.24, bf16[640,1152]{1,0:T(8,128)(2,1)S(1)} %collective-permute-done.3, f32[640]{0:T(1024)S(1)} %add_sqrt_fusion.1, bf16[640,1152]{1,0:T(8,128)(2,1)S(1)} %copy-done.1, f32[]{:T(128)} %bitcast.16, s32[640]{0:T(1024)S(1)} %collective-permute-done.2, ...), kind=kOutput, calls=%fused_computation.25 | convolution fusion | flops 951254400 | bytes 4597768 | tf_op jit(solution)/shard_map/dot_general | solution.py:19
  113.2 1.8 convolution_convert_fusion.1
  115.4 2.4 %multiply_reduce_fusion.1 = (f32[640]{0:T(1024)S(1)}, f32[640,1152]{1,0:T(8,128)S(1)}) fusion(f32[640]{0:T(1024)S(1)} %add_sqrt_fusion.1, bf16[640,1152]{1,0:T(8,128)(2,1)S(1)} %copy-done.1, f32[640,1152]{1,0:T(8,128)S(1)} %fusion.11, f32[640,1152]{1,0:T(8,128)S(1)} %convolution_add_fusion.1, bf16[640,1152]{1,0:T(8,128)(2,1)S(1)} %collective-permute-done.3, ...), kind=kOutput, calls=%fused_computation.22 | convolution fusion | flops 951827840 | bytes 13445124 | tf_op jit(solution)/shard_map/dot_general | solution.py:23
  117.8 0.6 add_multiply_fusion.4
  118.5 2.2 %subtract_divide_fusion.1 = f32[640,1152]{1,0:T(8,128)} fusion(f32[640,1152]{1,0:T(8,128)S(1)} %get-tuple-element.12, f32[640]{0:T(1024)S(1)} %get-tuple-element.11, f32[640]{0:T(1024)S(1)} %add_sqrt_fusion.1, bf16[640,1152]{1,0:T(8,128)(2,1)S(1)} %copy-done.1), kind=kLoop, calls=%fused_computation.21 | loop fusion | flops 3686400 | bytes 7377920 | tf_op jit(solution)/shard_map/div | solution.py:54
  120.6 57.3 %collective-permute-done.7 = bf16[640,1152]{1,0:T(8,128)(2,1)S(1)} collective-permute-done((bf16[640,1152]{1,0:T(8,128)(2,1)S(1)}, bf16[640,1152]{1,0:T(8,128)(2,1)S(1)}, u32[]{:S(2)}, u32[]{:S(2)}) %collective-permute-start.7) | collective-permute-done | bytes 1474592 | tf_op jit(solution)/shard_map/ppermute | solution.py:9
  177.9 2.4 %multiply_reduce_fusion = (f32[640]{0:T(1024)S(1)}, f32[640,1152]{1,0:T(8,128)S(1)}) fusion(bf16[640,1152]{1,0:T(8,128)(2,1)S(1)} %collective-permute-done.8, bf16[640,1152]{1,0:T(8,128)(2,1)S(1)} %collective-permute-done.7, bf16[640,1152]{1,0:T(8,128)(2,1)S(1)} %collective-permute-done.6, f32[640]{0:T(1024)S(1)} %add_sqrt_fusion, ...), kind=kOutput, calls=%fused_computation.19 | convolution fusion | flops 958463360 | bytes 11973124 | tf_op jit(solution)/shard_map/dot_general | solution.py:24
  180.3 2.7 %subtract_divide_fusion = f32[640,1152]{1,0:T(8,128)} fusion(f32[640]{0:T(1024)S(1)} %get-tuple-element.13, f32[640]{0:T(1024)S(1)} %add_sqrt_fusion, bf16[640,1152]{1,0:T(8,128)(2,1)S(1)} %collective-permute-done.8, bf16[640,1152]{1,0:T(8,128)(2,1)S(1)} %collective-permute-done.7, f32[640,1152]{1,0:T(8,128)S(1)} %get-tuple-element.14, ...), kind=kLoop, calls=%fused_computation.18 | loop fusion | flops 8110080 | bytes 11801600 | tf_op jit(solution)/shard_map/div | solution.py:57
  (22 shorter events, 1.3 us)
Async XLA Ops:
  0.6 1.9 %copy-start = (bf16[640,1152]{1,0:T(8,128)(2,1)S(1)}, bf16[640,1152]{1,0:T(8,128)(2,1)}, u32[]{:S(2)}) copy-start(bf16[640,1152]{1,0:T(8,128)(2,1)} %param.7) | copy-start | bytes 4423684
  2.5 2.6 %copy-start.2 = (s32[640]{0:T(1024)S(1)}, s32[640]{0:T(1024)}, u32[]{:S(2)}) copy-start(s32[640]{0:T(1024)} %param.9) | copy-start | bytes 7684
  2.5 5.9 %copy-start.1 = (bf16[640,1152]{1,0:T(8,128)(2,1)S(1)}, bf16[640,1152]{1,0:T(8,128)(2,1)}, u32[]{:S(2)}) copy-start(bf16[640,1152]{1,0:T(8,128)(2,1)} %param.6) | copy-start | bytes 4423684
  2.5 7.5 %copy-start.3 = (s32[640]{0:T(1024)S(1)}, s32[640]{0:T(1024)}, u32[]{:S(2)}) copy-start(s32[640]{0:T(1024)} %param.8) | copy-start | bytes 7684
  3.0 41.4 %collective-permute-start.5 = (bf16[640,1152]{1,0:T(8,128)(2,1)S(1)}, bf16[640,1152]{1,0:T(8,128)(2,1)S(1)}, u32[]{:S(2)}, u32[]{:S(2)}) collective-permute-start(bf16[640,1152]{1,0:T(8,128)(2,1)S(1)} %fusion.9), channel_id=1, source_target_pairs={{0,1},{1,2},{2,3},{3,4},{4,5},{5,6},{6,7},{7,8},{8,9},{9,10},{10,1... | collective-permute-start | bytes 4423688 | tf_op jit(solution)/shard_map/ppermute | solution.py:9
  3.1 57.7 %collective-permute-start.1 = (bf16[640,1152]{1,0:T(8,128)(2,1)S(1)}, bf16[640,1152]{1,0:T(8,128)(2,1)S(1)}, u32[]{:S(2)}, u32[]{:S(2)}) collective-permute-start(bf16[640,1152]{1,0:T(8,128)(2,1)S(1)} %fusion.9), channel_id=1, source_target_pairs={{0,16},{16,32},{32,48},{48,64},{64,80},{80,96},{96,112},{112,128},... | collective-permute-start | bytes 4423688 | tf_op jit(solution)/shard_map/ppermute | solution.py:9
  5.1 39.3 %collective-permute-start.4 = (s32[640]{0:T(1024)S(1)}, s32[640]{0:T(1024)S(1)}, u32[]{:S(2)}, u32[]{:S(2)}) collective-permute-start(s32[640]{0:T(1024)S(1)} %copy-done.2), channel_id=1, source_target_pairs={{0,1},{1,2},{2,3},{3,4},{4,5},{5,6},{6,7},{7,8},{8,9},{9,10},{10,1... | collective-permute-start | bytes 7688 | tf_op jit(solution)/shard_map/ppermute | solution.py:9
  6.4 38.0 %collective-permute-start = (s32[640]{0:T(1024)S(1)}, s32[640]{0:T(1024)S(1)}, u32[]{:S(2)}, u32[]{:S(2)}) collective-permute-start(s32[640]{0:T(1024)S(1)} %copy-done.2), channel_id=1, source_target_pairs={{0,16},{16,32},{32,48},{48,64},{64,80},{80,96},{96,112},{112,128},... | collective-permute-start | bytes 7688 | tf_op jit(solution)/shard_map/ppermute | solution.py:9
  44.4 30.0 %collective-permute-start.2 = (s32[640]{0:T(1024)S(1)}, s32[640]{0:T(1024)S(1)}, u32[]{:S(2)}, u32[]{:S(2)}) collective-permute-start(s32[640]{0:T(1024)S(1)} %collective-permute-done), channel_id=1, source_target_pairs={{0,16},{16,32},{32,48},{48,64},{64,80},{80,96},{96,112},{112,128},... | collective-permute-start | bytes 7688 | tf_op jit(solution)/shard_map/ppermute | solution.py:9
  48.6 72.0 %collective-permute-start.8 = (bf16[640,1152]{1,0:T(8,128)(2,1)S(1)}, bf16[640,1152]{1,0:T(8,128)(2,1)S(1)}, u32[]{:S(2)}, u32[]{:S(2)}) collective-permute-start(bf16[640,1152]{1,0:T(8,128)(2,1)S(1)} %convolution_convert_fusion), channel_id=1, source_target_pairs={{0,15},{1,0},{2,1},{3,2},{4,3},{5,4},{6,5},{7,6},{8,7},{9,8},{10,9... | collective-permute-start | bytes 4423688 | tf_op jit(solution)/shard_map/ppermute | solution.py:9
  60.8 50.1 %collective-permute-start.3 = (bf16[640,1152]{1,0:T(8,128)(2,1)S(1)}, bf16[640,1152]{1,0:T(8,128)(2,1)S(1)}, u32[]{:S(2)}, u32[]{:S(2)}) collective-permute-start(bf16[640,1152]{1,0:T(8,128)(2,1)S(1)} %collective-permute-done.1), channel_id=1, source_target_pairs={{0,16},{16,32},{32,48},{48,64},{64,80},{80,96},{96,112},{112,128},... | collective-permute-start | bytes 4423688 | tf_op jit(solution)/shard_map/ppermute | solution.py:9
  65.0 55.7 %collective-permute-start.6 = (bf16[640,1152]{1,0:T(8,128)(2,1)S(1)}, bf16[640,1152]{1,0:T(8,128)(2,1)S(1)}, u32[]{:S(2)}, u32[]{:S(2)}) collective-permute-start(bf16[640,1152]{1,0:T(8,128)(2,1)S(1)} %convolution_convert_fusion.2), channel_id=1, source_target_pairs={{0,240},{16,0},{32,16},{48,32},{64,48},{80,64},{96,80},{112,96},{1... | collective-permute-start | bytes 4423688 | tf_op jit(solution)/shard_map/ppermute | solution.py:9
  115.1 62.9 %collective-permute-start.7 = (bf16[640,1152]{1,0:T(8,128)(2,1)S(1)}, bf16[640,1152]{1,0:T(8,128)(2,1)S(1)}, u32[]{:S(2)}, u32[]{:S(2)}) collective-permute-start(bf16[640,1152]{1,0:T(8,128)(2,1)S(1)} %convolution_convert_fusion.1), channel_id=1, source_target_pairs={{0,224},{16,240},{32,0},{48,16},{64,32},{80,48},{96,64},{112,80},{... | collective-permute-start | bytes 4423688 | tf_op jit(solution)/shard_map/ppermute | solution.py:9
where the time goes:
time: 183 us
  waiting for transfers between devices  124 us (68%)
  matrix products  24.5 us (13%)
  starting transfers between devices  24.1 us (13%)
  other arithmetic  8.13 us (4%)
  between operations  2.09 us (1%)
    ppermute x9, waiting for transfers between devices, passed_along(): lax.ppermute(shard, axis, [(i, (i + by) % devices) for i in range(devices)])  124 us
    ppermute x9, starting transfers between devices, passed_along(): lax.ppermute(shard, axis, [(i, (i + by) % devices) for i in range(devices)])  24.1 us
    dot_general x4, matrix products, tile_terms(): jnp.dot(image_bf, text_bf.T, preferred_element_type=jnp.float32)  9.35 us
    dot_general x4, matrix products, tile_terms(): lax.dot_general(coef, image_bf, (((0,), (0,)), ((), ())), preferred_eleme...  7.92 us
    dot_general x4, matrix products, tile_terms(): image_part = jnp.dot(coef, text_bf, preferred_element_type=jnp.float32)  7.27 us
  transfers between devices with their start and end apart: 9, of which 3 were waited for; matrix products, arithmetic and copies ran while one was open for 14% of the time, Pallas kernels for 0%

commit v1 on v0

v1 whole, which is shorter than its diff:
```python
import jax
import jax.numpy as jnp
from jax import lax
from jax.sharding import PartitionSpec as P


def passed_along(shard, axis, by):
    devices = lax.axis_size(axis)
    return lax.ppermute(shard, axis, [(i, (i + by) % devices) for i in range(devices)])


def unit_rows(values):
    full = values.astype(jnp.float32)
    norms = jnp.sqrt(jnp.sum(full * full, axis=-1, keepdims=True) + 1e-06)
    return (full / norms, norms)


def pair_terms(image_bf, image_ids, text_bf, text_ids, scale, bias):
    logits = scale * jnp.dot(image_bf, text_bf.T, preferred_element_type=jnp.float32) + bias
    signs = jnp.where(image_ids[:, None] == text_ids[None, :], 1.0, -1.0).astype(jnp.float32)
    score = -signs * logits
    coef = (-signs * scale * jax.nn.sigmoid(score)).astype(jnp.bfloat16)
    return score, coef


def image_side(coef, text_bf):
    return jnp.dot(coef, text_bf, preferred_element_type=jnp.float32)


def text_side(coef, image_bf):
    return lax.dot_general(coef, image_bf, (((0,), (0,)), ((), ())), preferred_element_type=jnp.float32)


def shards(images, texts, image_ids, text_ids, logit_scale, logit_bias):
    rows = images.shape[0]
    image_unit, image_norm = unit_rows(images)
    text_unit, text_norm = unit_rows(texts)
    image_bf = image_unit.astype(jnp.bfloat16)
    text_bf = text_unit.astype(jnp.bfloat16)
    scale = logit_scale[0]
    bias = logit_bias[0]
    near_text = passed_along(text_bf, "blk", 1)
    near_image = passed_along(image_bf, "blk", -1)
    hop_text = passed_along(text_bf, "group", 1)
    hop_image = passed_along(image_bf, "group", -1)
    near_tid = passed_along(text_ids, "blk", 1)
    near_iid = passed_along(image_ids, "blk", -1)
    hop_tid = passed_along(text_ids, "group", 1)
    hop_iid = passed_along(image_ids, "group", -1)
    far_tid = passed_along(text_ids, "blk", 2)
    far_iid = passed_along(image_ids, "blk", -2)
    far_text = passed_along(near_text, "blk", 1)
    far_image = passed_along(near_image, "blk", -1)

    score, coef = pair_terms(image_bf, image_ids, text_bf, text_ids, scale, bias)
    loss = jnp.sum(jax.nn.softplus(score), axis=1)
    image_unit_grad = image_side(coef, text_bf)
    text_unit_grad = text_side(coef, image_bf)
    for there, their_ids in ((near_text, near_tid), (hop_text, hop_tid), (far_text, far_tid)):
        score, coef = pair_terms(image_bf, image_ids, there, their_ids, scale, bias)
        loss = loss + jnp.sum(jax.nn.softplus(score), axis=1)
        image_unit_grad = image_unit_grad + image_side(coef, there)
    for there, their_ids in ((near_image, near_iid), (hop_image, hop_iid), (far_image, far_iid)):
        _, coef = pair_terms(there, their_ids, text_bf, text_ids, scale, bias)
        text_unit_grad = text_unit_grad + text_side(coef, there)
    row_loss = loss / (4 * rows)
    image_grad = (
        image_unit_grad - image_unit * jnp.sum(image_unit * image_unit_grad, axis=1, keepdims=True)
    ) / image_norm
    text_grad = (
        text_unit_grad - text_unit * jnp.sum(text_unit * text_unit_grad, axis=1, keepdims=True)
    ) / text_norm
    return (row_loss, image_grad, text_grad)


def solution(mesh):
    placed = (
        P(("blk", "group"), None),
        P(("blk", "group"), None),
        P(("blk", "group")),
        P(("blk", "group")),
        P(),
        P(),
    )
    return jax.shard_map(
        shards,
        mesh=mesh,
        in_specs=placed,
        out_specs=(P(("blk", "group")), P(("blk", "group"), None), P(("blk", "group"), None)),
        check_vma=False,
    )
```

time: 183 us -> 145 us (0.79)
  the two profiles are of different devices: /device:TPU:4 before, /device:TPU:13 now
where the time goes in v1:
time: 145 us
  matrix products  64.5 us (44%)
  starting transfers between devices  41.3 us (28%)
  waiting for transfers between devices  24.7 us (17%)
  other arithmetic  12.2 us (8%)
  between operations  2.03 us (1%)
    ppermute x12, starting transfers between devices, passed_along(): lax.ppermute(shard, axis, [(i, (i + by) % devices) for i in range(devices)])  41.3 us
    dot_general x4, matrix products, text_side(): lax.dot_general(coef, image_bf, (((0,), (0,)), ((), ())), preferred_eleme...  28.7 us
    ppermute x12, waiting for transfers between devices, passed_along(): lax.ppermute(shard, axis, [(i, (i + by) % devices) for i in range(devices)])  24.7 us
    dot_general x4, matrix products, image_side(): return jnp.dot(coef, text_bf, preferred_element_type=jnp.float32)  18.5 us
    dot_general x4, matrix products, pair_terms(): jnp.dot(image_bf, text_bf.T, preferred_element_type=jnp.float32)  17.3 us
    div x1, other arithmetic, shards(): (text_unit_grad - text_unit * jnp.sum(text_unit * text_unit_grad, axis=1,...  4.02 us
  transfers between devices with their start and end apart: 12, of which 2 were waited for; matrix products, arithmetic and copies ran while one was open for 43% of the time, Pallas kernels for 0%

profile of v1, /device:TPU:13, one launch (start us, length us, event | category | flops | bytes accessed | tf_op | source)
XLA Modules:
  0.0 144.7 jit_solution(15138071195331013607)
XLA Ops:
  0.6 1.8 %fusion = f32[640]{0:T(1024)S(1)} fusion(bf16[640,1152]{1,0:T(8,128)(2,1)} %param.6), kind=kLoop, calls=%fused_computation.14 | loop fusion | flops 2211200 | bytes 1477120 | tf_op jit(solution)/shard_map/reduce_sum | solution.py:14
  2.5 1.6 %fusion.51 = bf16[640,1152]{1,0:T(8,128)(2,1)} fusion(f32[640]{0:T(1024)S(1)} %add_sqrt_fusion.1, bf16[640,1152]{1,0:T(8,128)(2,1)S(1)} %copy-done.1), kind=kLoop, calls=%fused_computation.87 | loop fusion | flops 2211840 | bytes 2951680 | tf_op jit(solution)/shard_map/convert_element_type | solution.py:38
  4.1 7.3 %collective-permute-start.7 = (bf16[640,1152]{1,0:T(8,128)(2,1)}, bf16[640,1152]{1,0:T(8,128)(2,1)}, u32[]{:S(2)}, u32[]{:S(2)}) collective-permute-start(bf16[640,1152]{1,0:T(8,128)(2,1)} %fusion.51), channel_id=1, source_target_pairs={{0,240},{16,0},{32,16},{48,32},{64,48},{80,64},{96,80},{112,96},{1... | collective-permute-start | bytes 4423688 | tf_op jit(solution)/shard_map/ppermute | solution.py:9
  13.8 1.6 %fusion.52 = bf16[640,1152]{1,0:T(8,128)(2,1)} fusion(f32[640]{0:T(1024)S(1)} %add_sqrt_fusion, bf16[640,1152]{1,0:T(8,128)(2,1)S(1)} %copy-done), kind=kLoop, calls=%fused_computation.88 | loop fusion | flops 2211840 | bytes 2951680 | tf_op jit(solution)/shard_map/convert_element_type | solution.py:39
  15.4 1.2 collective-permute-start.1
  18.0 4.0 %fusion.2 = (f32[640]{0:T(1024)S(1)}, f32[640,640]{0,1:T(8,128)S(1)}) fusion(f32[]{:T(128)} %bitcast.36, bf16[640,1152]{1,0:T(8,128)(2,1)} %fusion.51, bf16[640,1152]{1,0:T(8,128)(2,1)} %fusion.52, f32[]{:T(128)} %bitcast.24, s32[640]{0:T(1024)S(1)} %copy-done.2, s32[640]{0:T(1024)S(1)} %copy-done.3), kind=kOutput, calls=%fused_computation.20 | convolution fusion | flops 949042560 | bytes 4595208 | tf_op jit(solution)/shard_map/dot_general | solution.py:19
  21.9 4.6 %fusion.54 = f32[640,1152]{1,0:T(8,128)} fusion(bf16[640,1152]{1,0:T(8,128)(2,1)} %fusion.52, f32[640,640]{0,1:T(8,128)S(1)} %get-tuple-element.8, f32[]{:T(128)} %bitcast.31, s32[640]{0:T(1024)S(1)} %copy-done.3, s32[640]{0:T(1024)S(1)} %copy-done.2), kind=kOutput, calls=%fused_computation.90 | convolution fusion | flops 947404800 | bytes 6067204 | tf_op jit(solution)/shard_map/dot_general | solution.py:27
  26.5 4.7 %fusion.53 = f32[640,1152]{1,0:T(8,128)} fusion(bf16[640,1152]{1,0:T(8,128)(2,1)} %fusion.51, f32[640,640]{0,1:T(8,128)S(1)} %get-tuple-element.8, f32[]{:T(128)} %bitcast.35, s32[640]{0:T(1024)S(1)} %copy-done.3, s32[640]{0:T(1024)S(1)} %copy-done.2), kind=kOutput, calls=%fused_computation.89 | convolution fusion | flops 947404800 | bytes 6067204 | tf_op jit(solution)/shard_map/dot_general | solution.py:31
  31.1 11.6 %collective-permute-done.6 = s32[640]{0:T(1024)S(1)} collective-permute-done((s32[640]{0:T(1024)S(1)}, s32[640]{0:T(1024)S(1)}, u32[]{:S(2)}, u32[]{:S(2)}) %collective-permute-start.6) | collective-permute-done | bytes 2592 | tf_op jit(solution)/shard_map/ppermute | solution.py:9
  42.8 18.6 %collective-permute-start.3 = (bf16[640,1152]{1,0:T(8,128)(2,1)}, bf16[640,1152]{1,0:T(8,128)(2,1)}, u32[]{:S(2)}, u32[]{:S(2)}) collective-permute-start(bf16[640,1152]{1,0:T(8,128)(2,1)} %fusion.52), channel_id=1, source_target_pairs={{0,1},{1,2},{2,3},{3,4},{4,5},{5,6},{6,7},{7,8},{8,9},{9,10},{10,1... | collective-permute-start | bytes 4423688 | tf_op jit(solution)/shard_map/ppermute | solution.py:9
  61.4 8.0 %convolution_add_fusion.2 = f32[640,1152]{1,0:T(8,128)} fusion(f32[640,1152]{1,0:T(8,128)} %fusion.53, bf16[640,1152]{1,0:T(8,128)(2,1)} %collective-permute-done.7, bf16[640,1152]{1,0:T(8,128)(2,1)} %fusion.52, s32[640]{0:T(1024)S(1)} %collective-permute-done.6, f32[]{:T(128)} %bitcast.39, f32[]{:T(128)} %bitcast.26, s32[640]{0:T(1024)S(1)} %copy-done.2), kind=kOutput, calls=%fused_computation.6 | convolution fusion | flops 1893089280 | bytes 8852488 | tf_op jit(solution)/shard_map/dot_general | solution.py:31
  69.4 6.7 %collective-permute-start.10 = (s32[640]{0:T(1024)S(1)}, s32[640]{0:T(1024)S(1)}, u32[]{:S(2)}, u32[]{:S(2)}) collective-permute-start(s32[640]{0:T(1024)S(1)} %copy-done.3), channel_id=1, source_target_pairs={{0,224},{16,240},{32,0},{48,16},{64,32},{80,48},{96,64},{112,80},{... | collective-permute-start | bytes 7688 | tf_op jit(solution)/shard_map/ppermute | solution.py:9
  77.0 4.1 %fusion.3 = (f32[640]{0:T(1024)S(1)}, f32[640,640]{0,1:T(8,128)S(1)}) fusion(f32[]{:T(128)} %bitcast.42, bf16[640,1152]{1,0:T(8,128)(2,1)} %fusion.51, bf16[640,1152]{1,0:T(8,128)(2,1)} %collective-permute-done.1, f32[]{:T(128)} %bitcast.34, s32[640]{0:T(1024)S(1)} %collective-permute-done, s32[640]{0:T(1024)S(1)} %copy-done.3), kind=kOutput, calls=%fused_computation.21 | convolution fusion | flops 949042560 | bytes 4595208 | tf_op jit(solution)/shard_map/dot_general | solution.py:19
  81.1 4.5 %convolution_add_fusion.5 = f32[640,1152]{1,0:T(8,128)} fusion(f32[640,1152]{1,0:T(8,128)S(1)} %copy-done.5, bf16[640,1152]{1,0:T(8,128)(2,1)} %collective-permute-done.1, f32[640,640]{0,1:T(8,128)S(1)} %get-tuple-element.10, f32[]{:T(128)} %bitcast.30, s32[640]{0:T(1024)S(1)} %copy-done.3, s32[640]{0:T(1024)S(1)} %collective-permute-done), kind=kOutput, calls=%fused_computation.9 | convolution fusion | flops 948142080 | bytes 9016324 | tf_op jit(solution)/shard_map/dot_general | solution.py:27
  85.7 4.5 %collective-permute-start.11 = (bf16[640,1152]{1,0:T(8,128)(2,1)}, bf16[640,1152]{1,0:T(8,128)(2,1)}, u32[]{:S(2)}, u32[]{:S(2)}) collective-permute-start(bf16[640,1152]{1,0:T(8,128)(2,1)} %collective-permute-done.7), channel_id=1, source_target_pairs={{0,240},{16,0},{32,16},{48,32},{64,48},{80,64},{96,80},{112,96},{1... | collective-permute-start | bytes 4423688 | tf_op jit(solution)/shard_map/ppermute | solution.py:9
  90.2 5.1 %fusion.4 = (f32[640]{0:T(1024)S(1)}, f32[640,640]{0,1:T(8,128)}) fusion(f32[]{:T(128)} %bitcast.41, bf16[640,1152]{1,0:T(8,128)(2,1)} %fusion.51, bf16[640,1152]{1,0:T(8,128)(2,1)} %collective-permute-done.3, f32[]{:T(128)} %bitcast.33, s32[640]{0:T(1024)S(1)} %collective-permute-done.2, s32[640]{0:T(1024)S(1)} %copy-done.3), kind=kOutput, calls=%fused_computation.22 | convolution fusion | flops 949042560 | bytes 4595208 | tf_op jit(solution)/shard_map/dot_general | solution.py:19
  95.3 8.0 %convolution_add_fusion.1 = f32[640,1152]{1,0:T(8,128)} fusion(f32[640,1152]{1,0:T(8,128)} %convolution_add_fusion.2, bf16[640,1152]{1,0:T(8,128)(2,1)} %collective-permute-done.9, bf16[640,1152]{1,0:T(8,128)(2,1)} %fusion.52, s32[640]{0:T(1024)S(1)} %collective-permute-done.8, f32[]{:T(128)} %bitcast.38, f32[]{:T(128)} %bitcast.27, s32[640]{0:T(1024)S(1)} %copy-done.2), kind=kOutput, calls=%fused_computation.5 | convolution fusion | flops 1893089280 | bytes 8852488 | tf_op jit(solution)/shard_map/dot_general | solution.py:31
  103.3 5.9 %convolution_add_fusion.4 = f32[640,1152]{1,0:T(8,128)} fusion(f32[640,1152]{1,0:T(8,128)} %convolution_add_fusion.5, bf16[640,1152]{1,0:T(8,128)(2,1)} %collective-permute-done.3, f32[640,640]{0,1:T(8,128)} %get-tuple-element.6, f32[]{:T(128)} %bitcast.29, s32[640]{0:T(1024)S(1)} %copy-done.3, s32[640]{0:T(1024)S(1)} %collective-permute-done.2), kind=kOutput, calls=%fused_computation.8 | convolution fusion | flops 948142080 | bytes 9016324 | tf_op jit(solution)/shard_map/dot_general | solution.py:27
  109.3 13.1 %collective-permute-done.11 = bf16[640,1152]{1,0:T(8,128)(2,1)} collective-permute-done((bf16[640,1152]{1,0:T(8,128)(2,1)}, bf16[640,1152]{1,0:T(8,128)(2,1)}, u32[]{:S(2)}, u32[]{:S(2)}) %collective-permute-start.11) | collective-permute-done | bytes 1474592 | tf_op jit(solution)/shard_map/ppermute | solution.py:9
  122.3 8.0 %multiply_reduce_fusion = (f32[640]{0:T(1024)S(1)}, f32[640,1152]{1,0:T(8,128)}) fusion(f32[640]{0:T(1024)S(1)} %add_sqrt_fusion, bf16[640,1152]{1,0:T(8,128)(2,1)S(1)} %copy-done, f32[640,1152]{1,0:T(8,128)} %convolution_add_fusion.1, bf16[640,1152]{1,0:T(8,128)(2,1)} %collective-permute-done.11, bf16[640,1152]{1,0:T(8,128)(2,1)} %fusion.52, ...), kind=kOutput, calls=%fused_computation.17 | convolution fusion | flops 1896037760 | bytes 10332168 | tf_op jit(solution)/shard_map/dot_general | solution.py:31
  130.4 4.0 %subtract_divide_fusion = f32[640,1152]{1,0:T(8,128)} fusion(f32[640,1152]{1,0:T(8,128)} %get-tuple-element.14, f32[640]{0:T(1024)S(1)} %get-tuple-element.13, f32[640]{0:T(1024)S(1)} %add_sqrt_fusion, bf16[640,1152]{1,0:T(8,128)(2,1)S(1)} %copy-done), kind=kLoop, calls=%fused_computation.16 | loop fusion | flops 3686400 | bytes 7377920 | tf_op jit(solution)/shard_map/div | solution.py:70
  134.4 4.1 %fusion.5 = (f32[640]{0:T(1024)S(1)}, f32[640,640]{0,1:T(8,128)S(1)}) fusion(f32[]{:T(128)} %bitcast.40, bf16[640,1152]{1,0:T(8,128)(2,1)} %fusion.51, bf16[640,1152]{1,0:T(8,128)(2,1)} %collective-permute-done.5, f32[]{:T(128)} %bitcast.32, s32[640]{0:T(1024)S(1)} %collective-permute-done.4, s32[640]{0:T(1024)S(1)} %copy-done.3), kind=kOutput, calls=%fused_computation.23 | convolution fusion | flops 949042560 | bytes 4595208 | tf_op jit(solution)/shard_map/dot_general | solution.py:19
  138.5 3.4 %multiply_reduce_fusion.1 = (f32[640]{0:T(1024)S(1)}, f32[640,1152]{1,0:T(8,128)S(1)}) fusion(f32[640]{0:T(1024)S(1)} %add_sqrt_fusion.1, bf16[640,1152]{1,0:T(8,128)(2,1)S(1)} %copy-done.1, f32[640,1152]{1,0:T(8,128)S(1)} %copy-done.4, bf16[640,1152]{1,0:T(8,128)(2,1)} %collective-permute-done.5, f32[640,640]{0,1:T(8,128)S(1)} %get-tuple-element.4, ...), kind=kOutput, calls=%fused_computation.19 | convolution fusion | flops 951090560 | bytes 10496004 | tf_op jit(solution)/shard_map/dot_general | solution.py:27
  141.9 2.2 %subtract_divide_fusion.1 = f32[640,1152]{1,0:T(8,128)} fusion(f32[640,1152]{1,0:T(8,128)S(1)} %get-tuple-element.12, f32[640]{0:T(1024)S(1)} %get-tuple-element.11, f32[640]{0:T(1024)S(1)} %add_sqrt_fusion.1, bf16[640,1152]{1,0:T(8,128)(2,1)S(1)} %copy-done.1), kind=kLoop, calls=%fused_computation.18 | loop fusion | flops 3686400 | bytes 7377920 | tf_op jit(solution)/shard_map/div | solution.py:67
  (33 shorter events, 3.9 us)
Async XLA Ops:
  0.6 1.9 %copy-start.1 = (bf16[640,1152]{1,0:T(8,128)(2,1)S(1)}, bf16[640,1152]{1,0:T(8,128)(2,1)}, u32[]{:S(2)}) copy-start(bf16[640,1152]{1,0:T(8,128)(2,1)} %param.6) | copy-start | bytes 4423684
  2.5 9.9 %copy-start.3 = (s32[640]{0:T(1024)S(1)}, s32[640]{0:T(1024)}, u32[]{:S(2)}) copy-start(s32[640]{0:T(1024)} %param.8) | copy-start | bytes 7684
  2.5 10.9 %copy-start = (bf16[640,1152]{1,0:T(8,128)(2,1)S(1)}, bf16[640,1152]{1,0:T(8,128)(2,1)}, u32[]{:S(2)}) copy-start(bf16[640,1152]{1,0:T(8,128)(2,1)} %param.7) | copy-start | bytes 4423684
  4.1 38.6 %collective-permute-start.7 = (bf16[640,1152]{1,0:T(8,128)(2,1)}, bf16[640,1152]{1,0:T(8,128)(2,1)}, u32[]{:S(2)}, u32[]{:S(2)}) collective-permute-start(bf16[640,1152]{1,0:T(8,128)(2,1)} %fusion.51), channel_id=1, source_target_pairs={{0,240},{16,0},{32,16},{48,32},{64,48},{80,64},{96,80},{112,96},{1... | collective-permute-start | bytes 4423688 | tf_op jit(solution)/shard_map/ppermute | solution.py:9
  11.4 83.9 %collective-permute-start.9 = (bf16[640,1152]{1,0:T(8,128)(2,1)}, bf16[640,1152]{1,0:T(8,128)(2,1)}, u32[]{:S(2)}, u32[]{:S(2)}) collective-permute-start(bf16[640,1152]{1,0:T(8,128)(2,1)} %fusion.51), channel_id=1, source_target_pairs={{0,15},{1,0},{2,1},{3,2},{4,3},{5,4},{6,5},{7,6},{8,7},{9,8},{10,9... | collective-permute-start | bytes 4423688 | tf_op jit(solution)/shard_map/ppermute | solution.py:9
  12.4 30.4 %collective-permute-start.6 = (s32[640]{0:T(1024)S(1)}, s32[640]{0:T(1024)S(1)}, u32[]{:S(2)}, u32[]{:S(2)}) collective-permute-start(s32[640]{0:T(1024)S(1)} %copy-done.3), channel_id=1, source_target_pairs={{0,240},{16,0},{32,16},{48,32},{64,48},{80,64},{96,80},{112,96},{1... | collective-permute-start | bytes 7688 | tf_op jit(solution)/shard_map/ppermute | solution.py:9
  13.1 82.2 %collective-permute-start.8 = (s32[640]{0:T(1024)S(1)}, s32[640]{0:T(1024)S(1)}, u32[]{:S(2)}, u32[]{:S(2)}) collective-permute-start(s32[640]{0:T(1024)S(1)} %copy-done.3), channel_id=1, source_target_pairs={{0,15},{1,0},{2,1},{3,2},{4,3},{5,4},{6,5},{7,6},{8,7},{9,8},{10,9... | collective-permute-start | bytes 7688 | tf_op jit(solution)/shard_map/ppermute | solution.py:9
  13.8 4.2 %copy-start.2 = (s32[640]{0:T(1024)S(1)}, s32[640]{0:T(1024)}, u32[]{:S(2)}) copy-start(s32[640]{0:T(1024)} %param.9) | copy-start | bytes 7684
  15.4 60.7 %collective-permute-start.1 = (bf16[640,1152]{1,0:T(8,128)(2,1)}, bf16[640,1152]{1,0:T(8,128)(2,1)}, u32[]{:S(2)}, u32[]{:S(2)}) collective-permute-start(bf16[640,1152]{1,0:T(8,128)(2,1)} %fusion.52), channel_id=1, source_target_pairs={{0,16},{16,32},{32,48},{48,64},{64,80},{80,96},{96,112},{112,128},... | collective-permute-start | bytes 4423688 | tf_op jit(solution)/shard_map/ppermute | solution.py:9
  42.8 26.6 %collective-permute-start = (s32[640]{0:T(1024)S(1)}, s32[640]{0:T(1024)S(1)}, u32[]{:S(2)}, u32[]{:S(2)}) collective-permute-start(s32[640]{0:T(1024)S(1)} %copy-done.2), channel_id=1, source_target_pairs={{0,16},{16,32},{32,48},{48,64},{64,80},{80,96},{96,112},{112,128},... | collective-permute-start | bytes 7688 | tf_op jit(solution)/shard_map/ppermute | solution.py:9
  42.8 42.9 %collective-permute-start.3 = (bf16[640,1152]{1,0:T(8,128)(2,1)}, bf16[640,1152]{1,0:T(8,128)(2,1)}, u32[]{:S(2)}, u32[]{:S(2)}) collective-permute-start(bf16[640,1152]{1,0:T(8,128)(2,1)} %fusion.52), channel_id=1, source_target_pairs={{0,1},{1,2},{2,3},{3,4},{4,5},{5,6},{6,7},{7,8},{8,9},{9,10},{10,1... | collective-permute-start | bytes 4423688 | tf_op jit(solution)/shard_map/ppermute | solution.py:9
  69.4 39.9 %collective-permute-start.10 = (s32[640]{0:T(1024)S(1)}, s32[640]{0:T(1024)S(1)}, u32[]{:S(2)}, u32[]{:S(2)}) collective-permute-start(s32[640]{0:T(1024)S(1)} %copy-done.3), channel_id=1, source_target_pairs={{0,224},{16,240},{32,0},{48,16},{64,32},{80,48},{96,64},{112,80},{... | collective-permute-start | bytes 7688 | tf_op jit(solution)/shard_map/ppermute | solution.py:9
  76.1 9.5 %collective-permute-start.2 = (s32[640]{0:T(1024)S(1)}, s32[640]{0:T(1024)S(1)}, u32[]{:S(2)}, u32[]{:S(2)}) collective-permute-start(s32[640]{0:T(1024)S(1)} %copy-done.2), channel_id=1, source_target_pairs={{0,1},{1,2},{2,3},{3,4},{4,5},{5,6},{6,7},{7,8},{8,9},{9,10},{10,1... | collective-permute-start | bytes 7688 | tf_op jit(solution)/shard_map/ppermute | solution.py:9
  77.0 4.1 %copy-start.5 = (f32[640,1152]{1,0:T(8,128)S(1)}, f32[640,1152]{1,0:T(8,128)}, u32[]{:S(2)}) copy-start(f32[640,1152]{1,0:T(8,128)} %fusion.54) | copy-start | bytes 8847364
  85.7 48.7 %collective-permute-start.4 = (s32[640]{0:T(1024)S(1)}, s32[640]{0:T(1024)S(1)}, u32[]{:S(2)}, u32[]{:S(2)}) collective-permute-start(s32[640]{0:T(1024)S(1)} %copy-done.2), channel_id=1, source_target_pairs={{0,32},{16,48},{32,64},{48,80},{64,96},{80,112},{96,128},{112,144}... | collective-permute-start | bytes 7688 | tf_op jit(solution)/shard_map/ppermute | solution.py:9
  85.7 36.7 %collective-permute-start.11 = (bf16[640,1152]{1,0:T(8,128)(2,1)}, bf16[640,1152]{1,0:T(8,128)(2,1)}, u32[]{:S(2)}, u32[]{:S(2)}) collective-permute-start(bf16[640,1152]{1,0:T(8,128)(2,1)} %collective-permute-done.7), channel_id=1, source_target_pairs={{0,240},{16,0},{32,16},{48,32},{64,48},{80,64},{96,80},{112,96},{1... | collective-permute-start | bytes 4423688 | tf_op jit(solution)/shard_map/ppermute | solution.py:9
  95.3 39.1 %collective-permute-start.5 = (bf16[640,1152]{1,0:T(8,128)(2,1)}, bf16[640,1152]{1,0:T(8,128)(2,1)}, u32[]{:S(2)}, u32[]{:S(2)}) collective-permute-start(bf16[640,1152]{1,0:T(8,128)(2,1)} %collective-permute-done.1), channel_id=1, source_target_pairs={{0,16},{16,32},{32,48},{48,64},{64,80},{80,96},{96,112},{112,128},... | collective-permute-start | bytes 4423688 | tf_op jit(solution)/shard_map/ppermute | solution.py:9
  134.4 4.1 %copy-start.4 = (f32[640,1152]{1,0:T(8,128)S(1)}, f32[640,1152]{1,0:T(8,128)}, u32[]{:S(2)}) copy-start(f32[640,1152]{1,0:T(8,128)} %convolution_add_fusion.4) | copy-start | bytes 8847364

commit v2 on v0

v2 whole, which is shorter than its diff:
```python
import functools

import jax
import jax.numpy as jnp
from jax import lax
from jax.experimental import pallas as pl
from jax.experimental.pallas import tpu as pltpu
from jax.sharding import PartitionSpec as P

WHOLE = pl.BlockSpec(memory_space=pltpu.VMEM)
SCALAR = pl.BlockSpec(memory_space=pltpu.SMEM)
ANYWHERE = pl.BlockSpec(memory_space=pl.ANY)
LANES = 128
ID_ROWS = 16
BAND = 320
PART = 160
F32, BF16 = jnp.float32, jnp.bfloat16
BOTH = ("blk", "group")


def routes(blks, groups):
    out = [[], [], [], []]
    for p in range(blks):
        for q in range(groups):
            here, up = p * groups + q, 1 if p % 2 == 0 else -1
            out[0].append((here, (p + up) % blks * groups + q))
            out[1].append((here, (p - up) % blks * groups + q))
            out[2].append((here, p * groups + (q + up) % groups))
            out[3].append((here, p * groups + (q - up) % groups))
    return out


def unit_rows(values):
    full = values.astype(F32)
    return full * lax.rsqrt(jnp.sum(full * full, axis=-1, keepdims=True) + 1e-06)


def projected(values, grad):
    full = values.astype(F32)
    scales = lax.rsqrt(jnp.sum(full * full, axis=-1, keepdims=True) + 1e-06)
    along = jnp.sum(full * grad, axis=1, keepdims=True)
    return grad * scales - full * (along * (scales * scales * scales))


def score_block(mine, theirs, my_ids, their_ids, scale, bias):
    dots = lax.dot_general(mine, theirs, (((1,), (1,)), ((), ())), preferred_element_type=F32)
    turn = jnp.where(my_ids == their_ids, -1.0, 1.0)
    power = jnp.exp(turn * (scale * dots + bias))
    whole = 1.0 + power
    coef = ((turn * scale) * (power * pl.reciprocal(whole, approx=True))).astype(BF16)
    return coef, power, whole


def softplus_sums(power, whole):
    values = jnp.where(power < 1e-3, power - 0.5 * power * power, jnp.log(whole))
    total = values[:, :LANES]
    for at in range(LANES, values.shape[1], LANES):
        total = total + values[:, at : at + LANES]
    return total


def bands(rows, size):
    return [slice(at, at + size) for at in range(0, rows, size)]


def id_row(packed, first, rows):
    at = packed.shape[0] - ID_ROWS
    return packed[at:, first : first + rows].astype(F32)[:1]


def even_blk():
    return lax.rem(lax.axis_index("blk"), 2) == 0


def prep_kernel(is_a, texts, images, text_ids, image_ids, packed, raw, sems):
    rows = raw.shape[0]
    texts_here = even_blk() if is_a else jnp.logical_not(even_blk())
    pieces = bands(rows, PART)

    @pl.when(texts_here)
    def _():
        for n, piece in enumerate(pieces):
            pltpu.make_async_copy(texts.at[piece], raw.at[piece], sems.at[n]).start()

    @pl.when(jnp.logical_not(texts_here))
    def _():
        for n, piece in enumerate(pieces):
            pltpu.make_async_copy(images.at[piece], raw.at[piece], sems.at[n]).start()

    ids = jnp.where(texts_here, text_ids[...].reshape(1, rows), image_ids[...].reshape(1, rows))
    packed[rows:] = jnp.zeros((ID_ROWS, packed.shape[1]), BF16)
    packed[rows:, :rows] = jnp.broadcast_to(ids.astype(F32), (ID_ROWS, rows)).astype(BF16)
    for n, piece in enumerate(pieces):
        pltpu.make_async_copy(texts.at[piece], raw.at[piece], sems.at[n]).wait()
        packed[piece] = unit_rows(raw[piece]).astype(BF16)


def add_band(mine, theirs, col, their_ids, sb, band):
    coef, power, whole = score_block(mine[band], theirs, col[band, :1], their_ids, sb[0], sb[1])
    return jnp.dot(coef, theirs, preferred_element_type=F32), softplus_sums(power, whole)


def own_kernel(a, b, sb, a_grad, b_grad, a_loss, b_loss, a_col, b_col):
    rows = a_grad.shape[0]
    a_row, b_row = id_row(a, 0, rows), id_row(b, 0, rows)
    a_col[...] = jnp.transpose(jnp.broadcast_to(a_row, (LANES, rows)))
    b_col[...] = jnp.transpose(jnp.broadcast_to(b_row, (LANES, rows)))
    for band in bands(rows, BAND):
        a_grad[band], a_loss[band] = add_band(a, b[:rows], a_col, b_row, sb, band)
    for band in bands(rows, BAND):
        b_grad[band], b_loss[band] = add_band(b, a[:rows], b_col, a_row, sb, band)


def gate_kernel(theirs, after, out):
    pass


def add_kernel(theirs, mine, col, sb, grad_in, loss_in, grad, loss):
    rows = grad.shape[0]
    their_ids = id_row(theirs, 0, rows)
    for band in bands(rows, BAND):
        more, losses = add_band(mine, theirs[:rows], col, their_ids, sb, band)
        grad[band] = grad_in[band] + more
        loss[band] = loss_in[band] + losses


def last_kernel(
    a_theirs, b_theirs, a, b, a_col, b_col, sb, a_grad, b_grad, a_loss, b_loss, a_raw, b_raw,
    image_grad, text_grad, row_loss, a_out, b_out, loss_scr, sems
):
    rows = a_grad.shape[0]
    even = even_blk()
    sides = (
        (0, a_theirs, a, a_col, a_grad, a_loss, a_raw, a_out, jnp.logical_not(even)),
        (1, b_theirs, b, b_col, b_grad, b_loss, b_raw, b_out, even),
    )
    for n, theirs, mine, col, grad, loss, raw, out, is_image in sides:
        their_ids = id_row(theirs, 0, rows)
        for band in bands(rows, BAND):
            more, losses = add_band(mine, theirs[:rows], col, their_ids, sb, band)
            losses = loss[band] + losses
            if n == 0:
                loss_scr[band] = losses
            else:
                loss_scr[band] = jnp.where(is_image, losses, loss_scr[band])
            out[band] = projected(raw[band], grad[band] + more)
            piece = band.start // BAND

            @pl.when(is_image)
            def _():
                pltpu.make_async_copy(out.at[band], image_grad.at[band], sems.at[n, piece]).start()

            @pl.when(jnp.logical_not(is_image))
            def _():
                pltpu.make_async_copy(out.at[band], text_grad.at[band], sems.at[n, piece]).start()

    row_loss[...] = (jnp.sum(jnp.transpose(loss_scr[...]), axis=0, keepdims=True) / (4 * rows)).reshape(rows)
    for n, _, _, _, _, _, _, out, _ in sides:
        for piece, band in enumerate(bands(rows, BAND)):
            pltpu.make_async_copy(out.at[band], image_grad.at[band], sems.at[n, piece]).wait()


def cost(rows, total, width, matmuls):
    return pl.CostEstimate(
        flops=matmuls * rows * total * width // 4, bytes_accessed=2 * total * width, transcendentals=2 * rows * total
    )


def in_vmem(array):
    return pltpu.with_memory_space_constraint(array, pltpu.VMEM)


def shards(images, texts, image_ids, text_ids, logit_scale, logit_bias):
    rows, width = images.shape
    packed_rows = rows + ID_ROWS
    params = pltpu.CompilerParams(vmem_limit_bytes=12 * 1024 * 1024)
    last_params = pltpu.CompilerParams(vmem_limit_bytes=18 * 1024 * 1024)
    sb = jnp.concatenate([logit_scale, logit_bias])
    grad = pltpu.VMEM((rows, width), F32)
    lanes = pltpu.VMEM((rows, LANES), F32)
    packed = pltpu.VMEM((packed_rows, width), BF16)
    raw = pltpu.VMEM((rows, width), BF16)
    a_blk, b_blk, a_group, b_group = routes(lax.axis_size("blk"), lax.axis_size("group"))

    def prep(is_a):
        return pl.pallas_call(
            functools.partial(prep_kernel, is_a),
            out_shape=(packed, raw),
            in_specs=[ANYWHERE, ANYWHERE, WHOLE, WHOLE],
            out_specs=[WHOLE] * 2,
            scratch_shapes=[pltpu.SemaphoreType.DMA((rows // PART,))],
            compiler_params=params,
            name="prep",
        )(texts, images, text_ids, image_ids)

    def gate(theirs, after):
        return pl.pallas_call(
            gate_kernel,
            out_shape=packed,
            in_specs=[ANYWHERE] * 2,
            out_specs=ANYWHERE,
            input_output_aliases={0: 0},
            compiler_params=params,
            name="gate",
        )(in_vmem(theirs), after)

    def add(theirs, mine, col, grad_in, loss_in, name):
        return pl.pallas_call(
            add_kernel,
            out_shape=(grad, lanes),
            in_specs=[WHOLE] * 3 + [SCALAR] + [WHOLE] * 2,
            out_specs=[WHOLE] * 2,
            input_output_aliases={4: 0, 5: 1},
            compiler_params=params,
            cost_estimate=cost(rows, rows, width, 2),
            name=name,
        )(in_vmem(theirs), in_vmem(mine), in_vmem(col), sb, in_vmem(grad_in), in_vmem(loss_in))

    a, a_raw = prep(True)
    a_near = lax.ppermute(a, BOTH, a_blk)
    b, b_raw = prep(False)
    b_near = lax.ppermute(b, BOTH, b_blk)
    a_hop = lax.ppermute(a, BOTH, a_group)
    b_hop = lax.ppermute(b, BOTH, b_group)
    a_grad, b_grad, a_loss, b_loss, a_col, b_col = pl.pallas_call(
        own_kernel,
        out_shape=(grad, grad, lanes, lanes, lanes, lanes),
        in_specs=[WHOLE] * 2 + [SCALAR],
        out_specs=[WHOLE] * 6,
        compiler_params=params,
        cost_estimate=cost(rows, rows, width, 4),
        name="own",
    )(in_vmem(a), in_vmem(b), sb)
    a_near = gate(a_near, a_loss)
    b_far = lax.ppermute(a_near, BOTH, b_blk)
    b_near = gate(b_near, a_near)
    a_far = lax.ppermute(b_near, BOTH, a_blk)
    a_grad, a_loss = add(a_near, a, a_col, a_grad, a_loss, "neara")
    b_grad, b_loss = add(b_near, b, b_col, b_grad, b_loss, "nearb")
    b_grad, b_loss = add(b_far, b, b_col, b_grad, b_loss, "farb")
    a_grad, a_loss = add(a_far, a, a_col, a_grad, a_loss, "fara")
    image_grad, text_grad, row_loss = pl.pallas_call(
        last_kernel,
        out_shape=(
            jax.ShapeDtypeStruct((rows, width), F32),
            jax.ShapeDtypeStruct((rows, width), F32),
            jax.ShapeDtypeStruct((rows,), F32),
        ),
        in_specs=[WHOLE] * 6 + [SCALAR] + [WHOLE] * 6,
        out_specs=[ANYWHERE, ANYWHERE, WHOLE],
        scratch_shapes=[
            pltpu.VMEM((rows, width), F32),
            pltpu.VMEM((rows, width), F32),
            pltpu.VMEM((rows, LANES), F32),
            pltpu.SemaphoreType.DMA((2, rows // BAND)),
        ],
        compiler_params=last_params,
        cost_estimate=cost(rows, rows, width, 4),
        name="last",
    )(
        in_vmem(b_hop), in_vmem(a_hop), in_vmem(a), in_vmem(b), in_vmem(a_col), in_vmem(b_col), sb, in_vmem(a_grad),
        in_vmem(b_grad), in_vmem(a_loss), in_vmem(b_loss), in_vmem(a_raw), in_vmem(b_raw)
    )
    return (row_loss, image_grad, text_grad)


def solution(mesh):
    placed = (
        P(("blk", "group"), None),
        P(("blk", "group"), None),
        P(("blk", "group")),
        P(("blk", "group")),
        P(),
        P(),
    )
    return jax.shard_map(
        shards,
        mesh=mesh,
        in_specs=placed,
        out_specs=(P(("blk", "group")), P(("blk", "group"), None), P(("blk", "group"), None)),
        check_vma=False,
    )
```

time: 183 us -> 126 us (0.69)
  the two profiles are of different devices: /device:TPU:4 before, /device:TPU:1 now
where the time goes in v2:
time: 126 us; the launch traced here: 125 us
  waiting for transfers between devices  60.3 us (48%)
  Pallas kernels  37.5 us (30%)
  starting transfers between devices  21.3 us (17%)
  local copies, waits for them, and re-layouts  4.11 us (3%)
  between operations  2.19 us (2%)
    ppermute x1, waiting for transfers between devices, shards(): b_far = lax.ppermute(a_near, BOTH, b_blk)  37.7 us
    pallas_call x4, Pallas kernels, add(): pl.pallas_call(add_kernel, out_shape=(grad, lanes), in_specs=[WHOLE] * 3...  16.4 us
    ppermute x1, waiting for transfers between devices, shards(): a_near = lax.ppermute(a, BOTH, a_blk)  14.6 us
    pallas_call x1, Pallas kernels, shards(): pl.pallas_call(last_kernel, out_shape=(jax.ShapeDtypeStruct((rows, width)...  11.5 us
    ppermute x1, starting transfers between devices, shards(): b_far = lax.ppermute(a_near, BOTH, b_blk)  8.77 us
    ppermute x1, starting transfers between devices, shards(): b_near = lax.ppermute(b, BOTH, b_blk)  7.39 us
    ppermute x1, waiting for transfers between devices, shards(): b_hop = lax.ppermute(b, BOTH, b_group)  7.28 us
    pallas_call x1, Pallas kernels, shards(): pl.pallas_call(own_kernel, out_shape=(grad, grad, lanes, lanes, lanes, la...  7.08 us
  transfers between devices with their start and end apart: 6, of which 4 were waited for; matrix products, arithmetic and copies ran while one was open for 0% of the time, Pallas kernels for 20%

profile of v2, /device:TPU:1, one launch (start us, length us, event | category | flops | bytes accessed | tf_op | source)
XLA Modules:
  0.0 125.5 jit_solution(20167395361118046)
XLA Ops:
  0.6 1.4 %copy-done = bf16[640,1152]{1,0:T(8,128)(2,1)S(1)} copy-done((bf16[640,1152]{1,0:T(8,128)(2,1)S(1)}, bf16[640,1152]{1,0:T(8,128)(2,1)}, u32[]{:S(2)}) %copy-start) | copy-done | bytes 1474584
  2.0 1.4 %copy-done.1 = bf16[640,1152]{1,0:T(8,128)(2,1)S(1)} copy-done((bf16[640,1152]{1,0:T(8,128)(2,1)S(1)}, bf16[640,1152]{1,0:T(8,128)(2,1)}, u32[]{:S(2)}) %copy-start.1) | copy-done | bytes 1474584
  3.4 0.7 copy-done.2
  4.1 0.7 copy-done.3
  4.8 1.3 %prep.3 = (bf16[656,1152]{1,0:T(8,128)(2,1)S(1)}, bf16[640,1152]{1,0:T(8,128)(2,1)S(1)}) custom-call(bf16[640,1152]{1,0:T(8,128)(2,1)S(1)} %copy-done, bf16[640,1152]{1,0:T(8,128)(2,1)S(1)} %copy-done.1, s32[640]{0:T(1024)S(1)} %copy-done.2, s32[640]{0:T(1024)S(1)} %copy-done.3), custom_call_target="tpu_custom_call" | custom-call | tf_op jit(solution)/shard_map/prep/pallas_call | solution.py:186
  6.1 2.5 %collective-permute-start.3 = (bf16[656,1152]{1,0:T(8,128)(2,1)S(1)}, bf16[656,1152]{1,0:T(8,128)(2,1)S(1)}, u32[]{:S(2)}, u32[]{:S(2)}) collective-permute-start(bf16[656,1152]{1,0:T(8,128)(2,1)S(1)} %get-tuple-element.25.a.mine), channel_id=1, source_target_pairs={{0,16},{1,17},{2,18},{3,19},{4,20},{5,21},{6,22},{7,23},{8,24},{9,... | collective-permute-start | bytes 4534280 | tf_op jit(solution)/shard_map/ppermute | solution.py:220
  8.6 1.3 %prep.2 = (bf16[656,1152]{1,0:T(8,128)(2,1)S(1)}, bf16[640,1152]{1,0:T(8,128)(2,1)S(1)}) custom-call(bf16[640,1152]{1,0:T(8,128)(2,1)S(1)} %copy-done, bf16[640,1152]{1,0:T(8,128)(2,1)S(1)} %copy-done.1, s32[640]{0:T(1024)S(1)} %copy-done.2, s32[640]{0:T(1024)S(1)} %copy-done.3), custom_call_target="tpu_custom_call" | custom-call | tf_op jit(solution)/shard_map/prep/pallas_call | solution.py:186
  9.9 7.4 %collective-permute-start.2 = (bf16[656,1152]{1,0:T(8,128)(2,1)S(1)}, bf16[656,1152]{1,0:T(8,128)(2,1)S(1)}, u32[]{:S(2)}, u32[]{:S(2)}) collective-permute-start(bf16[656,1152]{1,0:T(8,128)(2,1)S(1)} %get-tuple-element.24.b.mine), channel_id=1, source_target_pairs={{0,240},{1,241},{2,242},{3,243},{4,244},{5,245},{6,246},{7,247},{8... | collective-permute-start | bytes 4534280 | tf_op jit(solution)/shard_map/ppermute | solution.py:222
  18.6 0.1 pad_maximum_fusion.sb
  18.7 7.1 %own.1 = (f32[640,1152]{1,0:T(8,128)S(1)}, f32[640,1152]{1,0:T(8,128)S(1)}, f32[640,128]{1,0:T(8,128)S(1)}, f32[640,128]{1,0:T(8,128)S(1)}, f32[640,128]{1,0:T(8,128)S(1)}, /*index=5*/f32[640,128]{1,0:T(8,128)S(1)}) custom-call(bf16[656,1152]{1,0:T(8,128)(2,1)S(1)} %get-tuple-element.25.a.mine, bf16[656,1152]{1,0:T(8,128)(2,1)S(1)} %get-tuple-element.24.b.mine, ...), custom_call_target="tpu_custom_call" | custom-call | flops 471859200 | bytes 1474560 | tf_op jit(solution)/shard_map/own/pallas_call | solution.py:225
  25.8 14.6 %collective-permute-done.3.theirs = bf16[656,1152]{1,0:T(8,128)(2,1)S(1)} collective-permute-done((bf16[656,1152]{1,0:T(8,128)(2,1)S(1)}, bf16[656,1152]{1,0:T(8,128)(2,1)S(1)}, u32[]{:S(2)}, u32[]{:S(2)}) %collective-permute-start.3) | collective-permute-done | bytes 1511456 | tf_op jit(solution)/shard_map/ppermute | solution.py:220
  40.4 8.8 %collective-permute-start.5 = (bf16[656,1152]{1,0:T(8,128)(2,1)S(1)}, bf16[656,1152]{1,0:T(8,128)(2,1)S(1)}, u32[]{:S(2)}, u32[]{:S(2)}) collective-permute-start(bf16[656,1152]{1,0:T(8,128)(2,1)S(1)} %gate.2.after.theirs), channel_id=1, source_target_pairs={{0,240},{1,241},{2,242},{3,243},{4,244},{5,245},{6,246},{7,247},{8... | collective-permute-start | bytes 4534280 | tf_op jit(solution)/shard_map/ppermute | solution.py:235
  49.1 0.7 collective-permute-done.2.theirs
  49.8 0.0 collective-permute-start.4
  49.8 2.1 %collective-permute-start = (bf16[656,1152]{1,0:T(8,128)(2,1)S(1)}, bf16[656,1152]{1,0:T(8,128)(2,1)S(1)}, u32[]{:S(2)}, u32[]{:S(2)}) collective-permute-start(bf16[656,1152]{1,0:T(8,128)(2,1)S(1)} %get-tuple-element.24.b.mine), channel_id=1, source_target_pairs={{0,15},{1,0},{2,1},{3,2},{4,3},{5,4},{6,5},{7,6},{8,7},{9,8},{10,9... | collective-permute-start | bytes 4534280 | tf_op jit(solution)/shard_map/ppermute | solution.py:224
  51.9 0.5 collective-permute-start.1
  52.4 4.1 %neara.1 = (f32[640,1152]{1,0:T(8,128)S(1)}, f32[640,128]{1,0:T(8,128)S(1)}) custom-call(bf16[656,1152]{1,0:T(8,128)(2,1)S(1)} %gate.2.after.theirs, bf16[656,1152]{1,0:T(8,128)(2,1)S(1)} %get-tuple-element.25.a.mine, f32[640,128]{1,0:T(8,128)S(1)} %get-tuple-element.26.col.a_col, ...), custom_call_target="tpu_custom_call", output_to_operand_aliasing={{0}: (4, {}), {1}: (5, {})} | custom-call | flops 235929600 | bytes 1474560 | tf_op jit(solution)/shard_map/neara/pallas_call | solution.py:208
  56.5 4.1 %nearb.1 = (f32[640,1152]{1,0:T(8,128)S(1)}, f32[640,128]{1,0:T(8,128)S(1)}) custom-call(bf16[656,1152]{1,0:T(8,128)(2,1)S(1)} %gate.3.theirs, bf16[656,1152]{1,0:T(8,128)(2,1)S(1)} %get-tuple-element.24.b.mine, f32[640,128]{1,0:T(8,128)S(1)} %get-tuple-element.27.col.b_col, f32[2]{0:T(128)S(1)} %pad_maximum_fusion.sb, ...), custom_call_target="tpu_custom_call", output_to_operand_aliasing={{0}: (4, {}), {1}: (5, {})} | custom-call | flops 235929600 | bytes 1474560 | tf_op jit(solution)/shard_map/nearb/pallas_call | solution.py:208
  60.6 37.7 %collective-permute-done.5.theirs = bf16[656,1152]{1,0:T(8,128)(2,1)S(1)} collective-permute-done((bf16[656,1152]{1,0:T(8,128)(2,1)S(1)}, bf16[656,1152]{1,0:T(8,128)(2,1)S(1)}, u32[]{:S(2)}, u32[]{:S(2)}) %collective-permute-start.5) | collective-permute-done | bytes 1511456 | tf_op jit(solution)/shard_map/ppermute | solution.py:235
  98.4 4.1 %farb.1 = (f32[640,1152]{1,0:T(8,128)S(1)}, f32[640,128]{1,0:T(8,128)S(1)}) custom-call(bf16[656,1152]{1,0:T(8,128)(2,1)S(1)} %collective-permute-done.5.theirs, bf16[656,1152]{1,0:T(8,128)(2,1)S(1)} %get-tuple-element.24.b.mine, f32[640,128]{1,0:T(8,128)S(1)} %get-tuple-element.27.col.b_col, ...), custom_call_target="tpu_custom_call", output_to_operand_aliasing={{0}: (4, {}), {1}: (5, {})} | custom-call | flops 235929600 | bytes 1474560 | tf_op jit(solution)/shard_map/farb/pallas_call | solution.py:208
  102.5 4.1 %fara.1 = (f32[640,1152]{1,0:T(8,128)S(1)}, f32[640,128]{1,0:T(8,128)S(1)}) custom-call(bf16[656,1152]{1,0:T(8,128)(2,1)S(1)} %collective-permute-done.4.theirs, bf16[656,1152]{1,0:T(8,128)(2,1)S(1)} %get-tuple-element.25.a.mine, f32[640,128]{1,0:T(8,128)S(1)} %get-tuple-element.26.col.a_col, ...), custom_call_target="tpu_custom_call", output_to_operand_aliasing={{0}: (4, {}), {1}: (5, {})} | custom-call | flops 235929600 | bytes 1474560 | tf_op jit(solution)/shard_map/fara/pallas_call | solution.py:208
  106.5 7.3 %collective-permute-done.a_theirs = bf16[656,1152]{1,0:T(8,128)(2,1)S(1)} collective-permute-done((bf16[656,1152]{1,0:T(8,128)(2,1)S(1)}, bf16[656,1152]{1,0:T(8,128)(2,1)S(1)}, u32[]{:S(2)}, u32[]{:S(2)}) %collective-permute-start) | collective-permute-done | bytes 1511456 | tf_op jit(solution)/shard_map/ppermute | solution.py:224
  113.8 0.0 collective-permute-done.1.b_theirs
  113.8 11.5 %last.1 = (f32[640,1152]{1,0:T(8,128)}, f32[640,1152]{1,0:T(8,128)}, f32[640]{0:T(1024)}) custom-call(bf16[656,1152]{1,0:T(8,128)(2,1)S(1)} %collective-permute-done.a_theirs, bf16[656,1152]{1,0:T(8,128)(2,1)S(1)} %collective-permute-done.1.b_theirs, bf16[656,1152]{1,0:T(8,128)(2,1)S(1)} %get-tuple-element.25.a.mine, ...), custom_call_target="tpu_custom_call" | custom-call | flops 471859200 | bytes 1474560 | tf_op jit(solution)/shard_map/last/pallas_call | solution.py:242
  (7 shorter events, 0.0 us)
Async XLA Ops:
  0.6 1.4 %copy-start = (bf16[640,1152]{1,0:T(8,128)(2,1)S(1)}, bf16[640,1152]{1,0:T(8,128)(2,1)}, u32[]{:S(2)}) copy-start(bf16[640,1152]{1,0:T(8,128)(2,1)} %texts.3) | copy-start | bytes 4423684
  2.0 1.4 %copy-start.1 = (bf16[640,1152]{1,0:T(8,128)(2,1)S(1)}, bf16[640,1152]{1,0:T(8,128)(2,1)}, u32[]{:S(2)}) copy-start(bf16[640,1152]{1,0:T(8,128)(2,1)} %images.3) | copy-start | bytes 4423684
  3.4 0.7 copy-start.2
  4.1 0.7 copy-start.3
  6.1 34.3 %collective-permute-start.3 = (bf16[656,1152]{1,0:T(8,128)(2,1)S(1)}, bf16[656,1152]{1,0:T(8,128)(2,1)S(1)}, u32[]{:S(2)}, u32[]{:S(2)}) collective-permute-start(bf16[656,1152]{1,0:T(8,128)(2,1)S(1)} %get-tuple-element.25.a.mine), channel_id=1, source_target_pairs={{0,16},{1,17},{2,18},{3,19},{4,20},{5,21},{6,22},{7,23},{8,24},{9,... | collective-permute-start | bytes 4534280 | tf_op jit(solution)/shard_map/ppermute | solution.py:220
  9.9 39.9 %collective-permute-start.2 = (bf16[656,1152]{1,0:T(8,128)(2,1)S(1)}, bf16[656,1152]{1,0:T(8,128)(2,1)S(1)}, u32[]{:S(2)}, u32[]{:S(2)}) collective-permute-start(bf16[656,1152]{1,0:T(8,128)(2,1)S(1)} %get-tuple-element.24.b.mine), channel_id=1, source_target_pairs={{0,240},{1,241},{2,242},{3,243},{4,244},{5,245},{6,246},{7,247},{8... | collective-permute-start | bytes 4534280 | tf_op jit(solution)/shard_map/ppermute | solution.py:222
  40.4 58.0 %collective-permute-start.5 = (bf16[656,1152]{1,0:T(8,128)(2,1)S(1)}, bf16[656,1152]{1,0:T(8,128)(2,1)S(1)}, u32[]{:S(2)}, u32[]{:S(2)}) collective-permute-start(bf16[656,1152]{1,0:T(8,128)(2,1)S(1)} %gate.2.after.theirs), channel_id=1, source_target_pairs={{0,240},{1,241},{2,242},{3,243},{4,244},{5,245},{6,246},{7,247},{8... | collective-permute-start | bytes 4534280 | tf_op jit(solution)/shard_map/ppermute | solution.py:235
  49.8 52.6 %collective-permute-start.4 = (bf16[656,1152]{1,0:T(8,128)(2,1)S(1)}, bf16[656,1152]{1,0:T(8,128)(2,1)S(1)}, u32[]{:S(2)}, u32[]{:S(2)}) collective-permute-start(bf16[656,1152]{1,0:T(8,128)(2,1)S(1)} %gate.3.theirs), channel_id=1, source_target_pairs={{0,16},{1,17},{2,18},{3,19},{4,20},{5,21},{6,22},{7,23},{8,24},{9,... | collective-permute-start | bytes 4534280 | tf_op jit(solution)/shard_map/ppermute | solution.py:237
  49.8 64.0 %collective-permute-start = (bf16[656,1152]{1,0:T(8,128)(2,1)S(1)}, bf16[656,1152]{1,0:T(8,128)(2,1)S(1)}, u32[]{:S(2)}, u32[]{:S(2)}) collective-permute-start(bf16[656,1152]{1,0:T(8,128)(2,1)S(1)} %get-tuple-element.24.b.mine), channel_id=1, source_target_pairs={{0,15},{1,0},{2,1},{3,2},{4,3},{5,4},{6,5},{7,6},{8,7},{9,8},{10,9... | collective-permute-start | bytes 4534280 | tf_op jit(solution)/shard_map/ppermute | solution.py:224
  51.9 62.0 %collective-permute-start.1 = (bf16[656,1152]{1,0:T(8,128)(2,1)S(1)}, bf16[656,1152]{1,0:T(8,128)(2,1)S(1)}, u32[]{:S(2)}, u32[]{:S(2)}) collective-permute-start(bf16[656,1152]{1,0:T(8,128)(2,1)S(1)} %get-tuple-element.25.a.mine), channel_id=1, source_target_pairs={{0,1},{1,2},{2,3},{3,4},{4,5},{5,6},{6,7},{7,8},{8,9},{9,10},{10,1... | collective-permute-start | bytes 4534280 | tf_op jit(solution)/shard_map/ppermute | solution.py:223
